TPU v7x, 1024 devices: a whole 4x4x32 slice. The times are simulated.
1024 devices in a mesh: dom: 128 (over z, x_hi, core), seg: 8 (over x_lo, y).
Axes of the slice: x: 4 (x_hi: 2, x_lo: 2; x = x_hi * 2 + x_lo), y: 4, z: 32, core: 2. Of those that a mesh axis runs over, the one named last changes fastest.
Arguments:
- state: float32 [8192, 9, 64], P(('dom', 'seg'))
- counts: int32 [8192], P(('dom', 'seg')), may hold values from 16 to 64
- neighbours: int32 [8192, 26], P(('dom', 'seg')), may hold values from 0 to 191, as said below
- new_place: int32 [8192], P(('dom', 'seg')), may hold values from 0 to 63, as said below
Outputs:
- moved_state: float32 [8192, 9, 64], P(('dom', 'seg'))
- moved_density: float32 [8192, 64], P(('dom', 'seg'))
Inputs may be any that keep to these rules, and one draw needn't show every extreme that they name: `neighbours`: each row lists 26 distinct region indices in 0 to 191, never the block's own index 64 + k. `new_place`: within each domain range the 64 values are a permutation.
All inputs are finite; a program needn't handle non-finite values.
Results may differ from a plain program's by a relative error of at most 0.00002.
Values sent between devices are 32-bit elements; how exact they have to be, the bound alone decides.
A program may use at most 32 MiB of HBM per device.

v0:
```python
import math

import jax
import jax.numpy as jnp
from jax import lax
from jax.sharding import PartitionSpec as P

SIGMA = 21.0 / (16.0 * math.pi)
GAMMA_LESS = 2.0 / 3.0
STEP_DT = 0.1


def with_halo(block, sides, width):
    for axis, dim in sides:
        count = lax.axis_size(axis)
        forward = [(i, i + 1) for i in range(count - 1)]
        backward = [(target, source) for source, target in forward]
        low = lax.ppermute(
            lax.slice_in_dim(block, block.shape[dim] - width, None, axis=dim), axis, forward
        )
        high = lax.ppermute(lax.slice_in_dim(block, 0, width, axis=dim), axis, backward)
        block = jnp.concatenate([low, block, high], axis=dim)
    return block


def offsets(own_pos, far_pos):
    return own_pos[:, :, None] - far_pos[:, None, :]


def density_tile(own, far):
    diff = offsets(own[0:3], far[0:3])
    dist = jnp.sqrt(jnp.sum(diff * diff, axis=0))
    smooth = own[7][:, None]
    ratio = dist / smooth
    shell = jnp.maximum(1.0 - 0.5 * ratio, 0.0)
    kernel = SIGMA / smooth**3 * shell**4 * (1.0 + 2.0 * ratio)
    return jnp.sum(kernel * far[6][None, :], axis=1)


def slope(own, far):
    diff = offsets(own[0:3], far[0:3])
    dist = jnp.sqrt(jnp.sum(diff * diff, axis=0))
    smooth = 0.5 * (own[7][:, None] + far[7][None, :])
    ratio = dist / smooth
    shell = jnp.maximum(1.0 - 0.5 * ratio, 0.0)
    factor = -5.0 * SIGMA / smooth**5 * shell**3
    return (diff, factor)


def tensor_tile(own, far, far_vol):
    diff, factor = slope(own, far)
    weight = -factor * far_vol[None, :]
    pairs = ((0, 0), (1, 1), (2, 2), (0, 1), (0, 2), (1, 2))
    return jnp.stack([jnp.sum(weight * diff[a] * diff[b], axis=1) for a, b in pairs])


def corrected(tensor):
    return jnp.stack(
        [2.0 - tensor[0], 2.0 - tensor[1], 2.0 - tensor[2], -tensor[3], -tensor[4], -tensor[5]]
    )


def apply_sym(sym, vec):
    first = sym[0] * vec[0] + sym[3] * vec[1] + sym[4] * vec[2]
    second = sym[3] * vec[0] + sym[1] * vec[1] + sym[5] * vec[2]
    third = sym[4] * vec[0] + sym[5] * vec[1] + sym[2] * vec[2]
    return jnp.stack([first, second, third])


def momentum_tile(own, own_corr, own_press, far, far_corr, far_press):
    diff, factor = slope(own, far)
    scaled = diff * factor[None]
    grad_own = apply_sym(own_corr[:, :, None], scaled)
    grad_far = apply_sym(far_corr[:, None, :], scaled)
    mass_far = far[6][None, :]
    accel = -jnp.sum(
        mass_far[None]
        * (own_press[None, :, None] * grad_own + far_press[None, None, :] * grad_far),
        axis=2,
    )
    dvel = own[3:6][:, :, None] - far[3:6][:, None, :]
    heat = own_press * jnp.sum(mass_far * jnp.sum(dvel * grad_own, axis=0), axis=1)
    return (accel, heat)


def tile_of(region, index):
    tile = jnp.take(region, index, axis=0)
    if tile.ndim == 3:
        return jnp.moveaxis(tile, 0, 1).reshape(tile.shape[1], -1)
    return tile.reshape(-1)


def spread(values, slab):
    whole = lax.all_gather(values, "seg", axis=0, tiled=True)
    return with_halo(whole, (("dom", 0),), slab)


def local(state, counts, neighbours, new_place):
    blocks = state.shape[0]
    width = state.shape[2]
    groups = lax.axis_size("seg")
    slab = blocks * groups
    seg_index = lax.axis_index("seg")
    live = (jnp.arange(width, dtype=jnp.int32)[None, :] < counts[:, None]).astype(jnp.float32)
    base = jnp.concatenate([state[:, 0:6], (state[:, 6] * live)[:, None], state[:, 7:9]], axis=1)
    own_rows = seg_index * blocks + jnp.arange(blocks, dtype=jnp.int32)
    lists = jnp.concatenate([(slab + own_rows)[:, None], neighbours], axis=1)
    block_ids = jnp.arange(blocks, dtype=jnp.int32)
    region_state = spread(base, slab)

    def first(b):
        return density_tile(base[b], tile_of(region_state, lists[b]))

    rho = lax.map(first, block_ids) + (1.0 - live)
    vol = base[:, 6] / rho
    region_vol = spread(vol, slab)

    def second(b):
        return tensor_tile(base[b], tile_of(region_state, lists[b]), tile_of(region_vol, lists[b]))

    corr = jnp.moveaxis(corrected(jnp.moveaxis(lax.map(second, block_ids), 1, 0)), 0, 1)
    press = GAMMA_LESS * base[:, 8] / rho
    extra = jnp.concatenate([corr, press[:, None]], axis=1)
    region_extra = spread(extra, slab)

    def third(b):
        far_extra = tile_of(region_extra, lists[b])
        return momentum_tile(
            base[b],
            corr[b],
            press[b],
            tile_of(region_state, lists[b]),
            far_extra[0:6],
            far_extra[6],
        )

    accel, heat = lax.map(third, block_ids)
    accel = accel * live[:, None]
    heat = heat * live
    velocity = state[:, 3:6] + STEP_DT * accel
    position = state[:, 0:3] + STEP_DT * velocity
    energy = state[:, 8] + STEP_DT * heat
    updated = jnp.concatenate([position, velocity, state[:, 6:8], energy[:, None]], axis=1)
    place_float = new_place.astype(jnp.float32)
    all_state, all_rho, all_place = (
        lax.all_gather(updated, "seg", axis=0, tiled=True),
        lax.all_gather(rho, "seg", axis=0, tiled=True),
        lax.all_gather(place_float, "seg", axis=0, tiled=True),
    )
    wanted = all_place.astype(jnp.int32)
    source = jnp.sum(
        jnp.where(
            wanted[None, :] == own_rows[:, None], jnp.arange(slab, dtype=jnp.int32)[None, :], 0
        ),
        axis=1,
    )
    return (jnp.take(all_state, source, axis=0), jnp.take(all_rho, source, axis=0))


def solution(mesh):
    return jax.shard_map(
        local,
        mesh=mesh,
        in_specs=(
            P(("dom", "seg"), None, None),
            P(("dom", "seg")),
            P(("dom", "seg"), None),
            P(("dom", "seg")),
        ),
        out_specs=(P(("dom", "seg"), None, None), P(("dom", "seg"), None)),
        check_vma=False,
    )
```

profile of v0, /device:TPU:1, one launch (start us, length us, event | category | flops | bytes accessed | tf_op | source)
XLA Modules:
  0.0 338.2 jit_solution(18310473332078634542)
XLA Ops:
  0.6 0.8 fusion.34
  1.4 0.7 slice.211
  2.1 0.8 fusion.30
  2.9 23.5 %all_gather.19 = f32[64,9,64]{2,0,1:T(8,128)S(1)} all-gather(f32[8,9,64]{2,0,1:T(8,128)S(1)} %pad_maximum_fusion.4), channel_id=1, replica_groups=mesh['dom'=128,'seg'=8] {'seg'}, dimensions={0}, use_global_device_ids=true | all-gather | bytes 165888 | tf_op jit(solution)/shard_map/all_gather | solution.py:94
  26.4 22.8 %collective-permute-start.1 = (f32[64,9,64]{2,0,1:T(8,128)S(1)}, f32[64,9,64]{2,0,1:T(8,128)S(1)}, u32[]{:S(2)}, u32[]{:S(2)}) collective-permute-start(f32[64,9,64]{2,0,1:T(8,128)S(1)} %all_gather.19), channel_id=1, source_target_pairs={{8,0},{16,8},{24,16},{32,24},{40,32},{48,40},{56,48},{64,56},{72,6... | collective-permute-start | bytes 442376 | tf_op jit(solution)/shard_map/ppermute | solution.py:21
  49.2 1.9 collective-permute-start
  51.1 1.3 dynamic-slice
  53.1 0.8 convert_dynamic-update-slice_fusion
  53.8 12.7 %all-reduce = f32[64]{0:T(128)S(1)} all-reduce(f32[64]{0:T(128)S(1)} %convert_dynamic-update-slice_fusion), channel_id=1, replica_groups=mesh['dom'=128,'seg'=8] {'seg'}, use_global_device_ids=true, to_apply=%add | all-reduce | flops 64 | bytes 512
  66.8 0.7 fusion.29
  67.8 0.8 pad_add_fusion
  69.1 0.9 copy.61
  70.0 35.3 %while.32 = (s32[]{:T(128)}, f32[8,64]{1,0:T(8,128)S(1)}, s32[8]{0:T(128)S(1)}, f32[8,9,64]{2,1,0:T(8,128)S(1)}, s32[8,27]{1,0:T(8,128)S(1)}, /*index=5*/f32[192...) while((s32[]{:T(128)}, f32[8,64]{1,0:T(8,128)S(1)}, s32[8]{0:T(128)S(1)}, ...), condition=%wide.region_4.6_spmd, body=%wide.region_1.5_spmd.sunk | while | flops 2228712 | bytes 1322401 | solution.py:114
  70.0 0.7 dynamic_slice.66
  74.4 0.7 dynamic_slice.66
  78.8 0.7 dynamic_slice.66
  83.2 0.7 dynamic_slice.66
  87.7 0.7 dynamic_slice.66
  92.1 0.7 dynamic_slice.66
  96.5 0.7 dynamic_slice.66
  100.9 0.7 dynamic_slice.66
  105.4 21.7 %all_gather.20 = f32[64,64]{1,0:T(8,128)S(1)} all-gather(f32[8,64]{1,0:T(8,128)S(1)} %get-tuple-element.254), channel_id=1, replica_groups=mesh['dom'=128,'seg'=8] {'seg'}, dimensions={0}, use_global_device_ids=true | all-gather | bytes 18432 | tf_op jit(solution)/shard_map/all_gather | solution.py:94
  127.1 12.0 %collective-permute-start.3 = (f32[64,64]{1,0:T(8,128)S(1)}, f32[64,64]{1,0:T(8,128)S(1)}, u32[]{:S(2)}, u32[]{:S(2)}) collective-permute-start(f32[64,64]{1,0:T(8,128)S(1)} %all_gather.20), channel_id=1, source_target_pairs={{8,0},{16,8},{24,16},{32,24},{40,32},{48,40},{56,48},{64,56},{72,6... | collective-permute-start | bytes 49160 | tf_op jit(solution)/shard_map/ppermute | solution.py:21
  139.2 1.9 collective-permute-start.2
  141.1 21.7 %all_gather.23 = f32[64,64]{1,0:T(8,128)S(1)} all-gather(f32[8,64]{1,0:T(8,128)S(1)} %get-tuple-element.255), channel_id=1, replica_groups=mesh['dom'=128,'seg'=8] {'seg'}, dimensions={0}, use_global_device_ids=true | all-gather | bytes 18432 | tf_op jit(solution)/shard_map/all_gather | solution.py:147
  163.4 45.3 %while.33 = (s32[]{:T(128)}, f32[8,6,64]{2,0,1:T(8,128)S(1)}, s32[8]{0:T(128)S(1)}, f32[8,9,64]{2,1,0:T(8,128)S(1)}, s32[8,27]{1,0:T(8,128)S(1)}, /*index=5*/f32...) while((s32[]{:T(128)}, f32[8,6,64]{2,0,1:T(8,128)S(1)}, ...), condition=%wide.region_13.15_spmd, body=%wide.region_5.14_spmd.sunk | while | flops 4221689 | bytes 4039032 | solution.py:121
  163.4 0.7 dynamic_slice.68
  168.2 0.8 multiply_reduce_fusion.17
  169.1 0.7 dynamic_slice.68
  173.8 0.8 multiply_reduce_fusion.17
  174.8 0.7 dynamic_slice.68
  179.5 0.8 multiply_reduce_fusion.17
  180.4 0.7 dynamic_slice.68
  185.2 0.8 multiply_reduce_fusion.17
  186.1 0.7 dynamic_slice.68
  190.8 0.8 multiply_reduce_fusion.17
  191.8 0.7 dynamic_slice.68
  196.5 0.8 multiply_reduce_fusion.17
  197.4 0.7 dynamic_slice.68
  202.2 0.8 multiply_reduce_fusion.17
  203.1 0.7 dynamic_slice.68
  207.8 0.8 multiply_reduce_fusion.17
  208.8 22.1 %all_gather.21 = f32[64,7,64]{2,0,1:T(8,128)S(1)} all-gather(f32[8,7,64]{2,0,1:T(8,128)S(1)} %pad_maximum_fusion.6), channel_id=1, replica_groups=mesh['dom'=128,'seg'=8] {'seg'}, dimensions={0}, use_global_device_ids=true | all-gather | bytes 129024 | tf_op jit(solution)/shard_map/all_gather | solution.py:94
  231.0 15.8 %collective-permute-start.5 = (f32[64,7,64]{2,0,1:T(8,128)S(1)}, f32[64,7,64]{2,0,1:T(8,128)S(1)}, u32[]{:S(2)}, u32[]{:S(2)}) collective-permute-start(f32[64,7,64]{2,0,1:T(8,128)S(1)} %all_gather.21), channel_id=1, source_target_pairs={{8,0},{16,8},{24,16},{32,24},{40,32},{48,40},{56,48},{64,56},{72,6... | collective-permute-start | bytes 344072 | tf_op jit(solution)/shard_map/ppermute | solution.py:21
  246.7 1.9 collective-permute-start.4
  248.7 0.7 broadcast_select_fusion.2
  249.3 2.3 collective-permute-done.4
  252.1 61.7 %while.34 = (s32[]{:T(128)}, f32[8,3,64]{2,0,1:T(8,128)S(1)}, f32[8,64]{1,0:T(8,128)S(1)}, s32[8]{0:T(128)S(1)}, s32[8,27]{1,0:T(8,128)S(1)}, /*index=5*/f32[192...) while((s32[]{:T(128)}, f32[8,3,64]{2,0,1:T(8,128)S(1)}, ...), condition=%wide.region_19.21_spmd, body=%wide.region_14.20_spmd.sunk | while | flops 10425598 | bytes 13043228 | solution.py:137
  252.1 0.7 dynamic_slice.72
  256.5 0.6 gather_fusion.3
  259.8 0.7 dynamic_slice.72
  264.2 0.6 gather_fusion.3
  267.5 0.7 dynamic_slice.72
  275.2 0.7 dynamic_slice.72
  279.6 0.6 gather_fusion.3
  282.9 0.7 dynamic_slice.72
  287.3 0.6 gather_fusion.3
  290.7 0.7 dynamic_slice.72
  298.4 0.7 dynamic_slice.72
  302.7 0.6 gather_fusion.3
  306.1 0.7 dynamic_slice.72
  310.4 0.6 gather_fusion.3
  313.9 22.9 %all_gather.22 = f32[64,9,64]{2,0,1:T(8,128)S(1)} all-gather(f32[8,9,64]{2,0,1:T(8,128)S(1)} %pad_maximum_fusion.5), channel_id=1, replica_groups=mesh['dom'=128,'seg'=8] {'seg'}, dimensions={0}, use_global_device_ids=true | all-gather | bytes 165888 | tf_op jit(solution)/shard_map/all_gather | solution.py:146
  337.6 0.6 copy.67
  (636 shorter events, 66.3 us)
Async XLA Ops:
  26.4 42.2 %collective-permute-start.1 = (f32[64,9,64]{2,0,1:T(8,128)S(1)}, f32[64,9,64]{2,0,1:T(8,128)S(1)}, u32[]{:S(2)}, u32[]{:S(2)}) collective-permute-start(f32[64,9,64]{2,0,1:T(8,128)S(1)} %all_gather.19), channel_id=1, source_target_pairs={{8,0},{16,8},{24,16},{32,24},{40,32},{48,40},{56,48},{64,56},{72,6... | collective-permute-start | bytes 442376 | tf_op jit(solution)/shard_map/ppermute | solution.py:21
  49.2 19.5 %collective-permute-start = (f32[64,9,64]{2,0,1:T(8,128)S(1)}, f32[64,9,64]{2,0,1:T(8,128)S(1)}, u32[]{:S(2)}, u32[]{:S(2)}) collective-permute-start(f32[64,9,64]{2,0,1:T(8,128)S(1)} %all_gather.19), channel_id=1, source_target_pairs={{0,8},{8,16},{16,24},{24,32},{32,40},{40,48},{48,56},{56,64},{64,7... | collective-permute-start | bytes 442376 | tf_op jit(solution)/shard_map/ppermute | solution.py:18
  70.0 35.4 %copy-start = (f32[8,9,64]{2,0,1:T(8,128)S(1)}, f32[8,9,64]{2,0,1:T(8,128)}, u32[]{:S(2)}) copy-start(f32[8,9,64]{2,0,1:T(8,128)} %param.12) | copy-start | bytes 55300
  70.0 35.4 %copy-start.1 = (s32[8]{0:T(128)S(1)}, s32[8]{0:T(128)}, u32[]{:S(2)}) copy-start(s32[8]{0:T(128)} %param.13) | copy-start | bytes 100
  127.1 36.3 %collective-permute-start.3 = (f32[64,64]{1,0:T(8,128)S(1)}, f32[64,64]{1,0:T(8,128)S(1)}, u32[]{:S(2)}, u32[]{:S(2)}) collective-permute-start(f32[64,64]{1,0:T(8,128)S(1)} %all_gather.20), channel_id=1, source_target_pairs={{8,0},{16,8},{24,16},{32,24},{40,32},{48,40},{56,48},{64,56},{72,6... | collective-permute-start | bytes 49160 | tf_op jit(solution)/shard_map/ppermute | solution.py:21
  139.2 24.2 %collective-permute-start.2 = (f32[64,64]{1,0:T(8,128)S(1)}, f32[64,64]{1,0:T(8,128)S(1)}, u32[]{:S(2)}, u32[]{:S(2)}) collective-permute-start(f32[64,64]{1,0:T(8,128)S(1)} %all_gather.20), channel_id=1, source_target_pairs={{0,8},{8,16},{16,24},{24,32},{32,40},{40,48},{48,56},{56,64},{64,7... | collective-permute-start | bytes 49160 | tf_op jit(solution)/shard_map/ppermute | solution.py:18
  231.0 18.4 %collective-permute-start.5 = (f32[64,7,64]{2,0,1:T(8,128)S(1)}, f32[64,7,64]{2,0,1:T(8,128)S(1)}, u32[]{:S(2)}, u32[]{:S(2)}) collective-permute-start(f32[64,7,64]{2,0,1:T(8,128)S(1)} %all_gather.21), channel_id=1, source_target_pairs={{8,0},{16,8},{24,16},{32,24},{40,32},{48,40},{56,48},{64,56},{72,6... | collective-permute-start | bytes 344072 | tf_op jit(solution)/shard_map/ppermute | solution.py:21
  246.7 4.9 %collective-permute-start.4 = (f32[64,7,64]{2,0,1:T(8,128)S(1)}, f32[64,7,64]{2,0,1:T(8,128)S(1)}, u32[]{:S(2)}, u32[]{:S(2)}) collective-permute-start(f32[64,7,64]{2,0,1:T(8,128)S(1)} %all_gather.21), channel_id=1, source_target_pairs={{0,8},{8,16},{16,24},{24,32},{32,40},{40,48},{48,56},{56,64},{64,7... | collective-permute-start | bytes 344072 | tf_op jit(solution)/shard_map/ppermute | solution.py:18
where the time goes:
time: 345 us; the launch traced here: 338 us
  blocking collectives  125 us (36%)
  local copies, waits for them, and re-layouts  61.7 us (18%)
  starting transfers between devices  56.4 us (16%)
  loops' own time  53 us (15%)
  other arithmetic  38.6 us (11%)
    all_gather x3, blocking collectives, spread(): whole = lax.all_gather(values, 'seg', axis=0, tiled=True)  67.3 us
    ppermute x3, starting transfers between devices, with_halo(): lax.ppermute(lax.slice_in_dim(block, 0, width, axis=dim), axis, backward)  50.6 us
    gather x40, local copies, waits for them, and re-layouts, tile_of(): tile = jnp.take(region, index, axis=0)  23.2 us
    all_gather x1, blocking collectives, local(): lax.all_gather(updated, 'seg', axis=0, tiled=True)  22.9 us
    all_gather x1, blocking collectives, local(): lax.all_gather(rho, 'seg', axis=0, tiled=True)  21.7 us
    another operation x1, loops' own time, local(): accel, heat = lax.map(third, block_ids)  18.2 us
    another operation x1, loops' own time, local(): lax.map(second, block_ids)  17.5 us
    another operation x1, loops' own time, local(): rho = lax.map(first, block_ids) + (1.0 - live)  17.3 us
  transfers between devices with their start and end apart: 6, of which 1 were waited for; matrix products, arithmetic and copies ran while one was open for 2% of the time, Pallas kernels for 0%

commit v1 on v0

v1 whole, which is shorter than its diff:
```python
import functools
import math

import jax
import jax.numpy as jnp
from jax import lax
from jax.experimental import pallas as pl
from jax.experimental.pallas import tpu as pltpu
from jax.sharding import PartitionSpec as P

SIGMA = 21.0 / (16.0 * math.pi)
SLOPE = -5.0 * 32.0 * SIGMA
GAMMA_LESS = 2.0 / 3.0
STEP_DT = 0.1
MESH = pl.DeviceIdType.MESH
F32 = jnp.float32
BF16 = jnp.bfloat16
SPLITS = 3
TINY = 1e-36


def split(value):
    parts = []
    for k in range(SPLITS):
        part = value.astype(BF16)
        parts.append(part)
        if k + 1 < SPLITS:
            value = value - part.astype(F32)
    return parts


def kernel(
    dims,
    state_ref,
    nb_ref,
    counts_ref,
    place_ref,
    out_ref,
    rho_ref,
    meta,
    pack_a,
    pack_b,
    pack_c,
    reg_m,
    reg_a,
    reg_b,
    reg_c,
    table,
    table_smem,
    far,
    far1,
    own_wide,
    weights,
    own_e,
    sums,
    res_l,
    res_m,
    res_q,
    moment,
    copy_sem,
    send_m,
    recv_m,
    send_a,
    recv_a,
    send_b,
    recv_b,
    send_c,
    recv_c,
):
    D, G, NBR = dims
    B = 8
    HALF = B // 2
    W = 64
    SLAB = G * B
    TILES = (NBR + 2) // 2
    SELF, PAD, PLACE, COUNT, TABLE0 = NBR, NBR + 1, 28, 29, 64
    dom = lax.axis_index("dom")
    seg = lax.axis_index("seg")

    def target(delta, o):
        return (lax.rem(dom + delta + D, D), lax.rem(seg + o, G))

    def each_peer(action):
        for delta in (-1, 1):

            def outer(o, c, delta=delta):
                action(delta, o)
                return c

            lax.fori_loop(0, G, outer, 0)

        def inner(o, c):
            action(0, o)
            return c

        lax.fori_loop(1, G, inner, 0)

    barrier = pltpu.get_barrier_semaphore()

    def greet(delta, o):
        pl.semaphore_signal(barrier, inc=1, device_id=target(delta, o), device_id_type=MESH)

    each_peer(greet)

    rows = lax.broadcasted_iota(jnp.int32, (B, 128), 0)
    lanes = lax.broadcasted_iota(jnp.int32, (B, 128), 1)
    low = lanes < W

    note = jnp.where(lanes == SELF, SLAB + seg * B + rows, 0)
    note = jnp.where(lanes == PAD, 3 * SLAB, note)
    for b in range(B):
        mine = rows == b
        note = jnp.where(mine & (lanes == PLACE), place_ref[b], note)
        note = jnp.where(mine & (lanes == COUNT), counts_ref[b], note)
        note = jnp.where((rows == 0) & (lanes == TABLE0 + seg * B + b), place_ref[b], note)
    meta[...] = note
    meta[:, 0:NBR] = nb_ref[...]
    for p in range(HALF):
        pair = jnp.concatenate([state_ref[p, 0:8, :], state_ref[p + HALF, 0:8, :]], axis=1)
        limit = jnp.where(low, counts_ref[p], counts_ref[p + HALF] + W)
        pack_a[p] = jnp.where((rows == 6) & (lanes >= limit), 0.0, pair)
        pack_a[HALF, p : p + 1] = jnp.concatenate(
            [state_ref[p, 8:9, :], state_ref[p + HALF, 8:9, :]], axis=1
        )
        pack_a[HALF, p + HALF : p + HALF + 1] = jnp.concatenate(
            [state_ref[p, 6:7, :], state_ref[p + HALF, 6:7, :]], axis=1
        )

    pl.semaphore_wait(barrier, 3 * G - 1)

    def sent(src, dst, send_sem, recv_sem):
        def make(delta, o):
            slot = (1 - delta) * G + seg
            return pltpu.make_async_remote_copy(
                src_ref=src(delta),
                dst_ref=dst(slot, delta),
                send_sem=send_sem.at[(1 + delta) * G + o],
                recv_sem=recv_sem.at[slot],
                device_id=target(delta, o),
                device_id_type=MESH,
            )

        def take(delta, o):
            slot = (1 + delta) * G + lax.rem(seg + o, G)
            return pltpu.make_async_remote_copy(
                src_ref=src(delta),
                dst_ref=dst(slot, delta),
                send_sem=send_sem.at[(1 + delta) * G + o],
                recv_sem=recv_sem.at[slot],
                device_id=target(delta, o),
                device_id_type=MESH,
            )

        return (
            lambda: each_peer(lambda delta, o: make(delta, o).start()),
            lambda: each_peer(lambda delta, o: take(delta, o).wait_recv()),
            lambda: each_peer(lambda delta, o: make(delta, o).wait_send()),
        )

    meta_go, meta_in, meta_out = sent(
        lambda d: meta, lambda s, d: reg_m.at[s], send_m, recv_m
    )
    a_go, a_in, a_out = sent(
        lambda d: pack_a if d == 0 else pack_a.at[0:HALF],
        lambda s, d: reg_a.at[s] if d == 0 else reg_a.at[s, 0:HALF],
        send_a,
        recv_a,
    )
    b_go, b_in, b_out = sent(lambda d: pack_b, lambda s, d: reg_b.at[s], send_b, recv_b)
    c_go, c_in, c_out = sent(lambda d: pack_c, lambda s, d: reg_c.at[s], send_c, recv_c)

    meta_go()
    a_go()

    here = G + seg
    reg_m[here] = meta[...]
    reg_a[here] = pack_a[...]
    none = 3 * G
    zero = jnp.zeros((8, 128), F32)
    reg_b[none] = zero
    for p in range(HALF):
        reg_a[none, p] = zero
        reg_c[none, p] = zero
    reg_a[none, HALF] = zero

    meta_in()
    lists = jnp.zeros((B, 128), jnp.int32)
    notes = [reg_m[G + d] for d in range(G)]
    places = [jnp.broadcast_to(note[:, PLACE : PLACE + 1], (B, 128)) for note in notes]
    for b in range(B):
        found = jnp.zeros((B, 128), jnp.int32)
        for d in range(G):
            found = found + jnp.where(places[d] == seg * B + b, notes[d], 0)
        for shift in (4, 2, 1):
            found = found + pltpu.roll(found, shift, 0)
        lists = jnp.where(rows == b, found, lists)
    spread = []
    for q in range(3):
        total = reg_m[q * G, 0:1, :]
        for d in range(1, G):
            total = total + reg_m[q * G + d, 0:1, :]
        total = jnp.broadcast_to(total, (B, 128))
        spread.append(jnp.where(low, pltpu.roll(total, W, 1), total))
    first = jnp.where(low, spread[0], spread[1]) if SLAB == W else None
    if SLAB == W:
        inside = lists & 127
        placed = jnp.where(
            lists < 128,
            jnp.take_along_axis(first, inside, axis=1, mode="promise_in_bounds"),
            jnp.take_along_axis(spread[2], inside, axis=1, mode="promise_in_bounds"),
        )
        moved = jnp.where(lists < 3 * SLAB, (lists & (-SLAB)) + placed, lists)
    else:
        moved = lists
        inside = lists & (SLAB - 1)
        for q in range(3):
            got = jnp.take_along_axis(spread[q], inside, axis=1, mode="promise_in_bounds")
            moved = jnp.where((lists >= q * SLAB) & (lists < (q + 1) * SLAB), q * SLAB + got, moved)
    inside = jnp.clip(lists, 0, 3 * SLAB)
    moved = jnp.clip(moved, 0, 3 * SLAB)
    half = (inside >> 2) & 1
    table[0] = (((inside >> 3) * (HALF + 1) + (inside & 3)) << 1) | half
    table[1] = (((moved >> 3) * HALF + (moved & 3)) << 1) | ((moved >> 2) & 1)
    live = jnp.where(lanes < jnp.broadcast_to(lists[:, COUNT : COUNT + 1], (B, 128)), 1.0, 0.0)
    to_smem = pltpu.make_async_copy(table, table_smem, copy_sem)
    to_smem.start()
    to_smem.wait()

    a_in()

    @pl.when(dom == 0)
    def _():
        for d in range(G):
            for p in range(HALF):
                reg_a[d, p] = zero

    @pl.when(dom == D - 1)
    def _():
        for d in range(G):
            for p in range(HALF):
                reg_a[2 * G + d, p] = zero

    def joined(which, b, t, load):
        even, odd = table_smem[which, b, 2 * t], table_smem[which, b, 2 * t + 1]
        left, right = load(even >> 1), load(odd >> 1)
        left = pltpu.roll(left, (even & 1) * W, 1)
        right = pltpu.roll(right, W - (odd & 1) * W, 1)
        mask = low if left.shape[0] == B else low[0:1]
        return jnp.where(mask, left, right)

    def load_a(tile):
        return reg_a[lax.div(tile, HALF + 1), lax.rem(tile, HALF + 1)]

    def load_b(row):
        return reg_b[row >> 2, pl.ds(row & 3, 1), :]

    def load_c(tile):
        return reg_c[tile >> 2, tile & 3]

    def density(b, c):
        own = joined(0, b, TILES - 1, load_a)
        where_own = table_smem[0, b, SELF]
        dev, pair = lax.div(where_own >> 1, HALF + 1), lax.rem(where_own >> 1, HALF + 1)
        shift = (where_own & 1) * W
        own_e[pl.ds(b, 1), :] = pltpu.roll(reg_a[dev, HALF, pl.ds(pair, 1), :], shift, 1)
        own_e[pl.ds(B + b, 1), :] = pltpu.roll(
            reg_a[dev, HALF, pl.ds(HALF + pair, 1), :], shift, 1
        )
        centre = jnp.sum(jnp.where(low, own, 0.0), axis=1, keepdims=True) * (1.0 / W)
        centre = jnp.where(rows < 6, jnp.broadcast_to(centre, (B, 128)), 0.0)
        turned = jnp.transpose(own)[0:W]
        for k, field in enumerate((0, 1, 2, 7)):
            own_wide[k] = jnp.broadcast_to(turned[:, field : field + 1], (W, 128))
        own_wide[4] = 0.5 / own_wide[3]

        def tile(t, acc):
            value = joined(0, b, t, load_a)
            far[pl.ds(pl.multiple_of((b * TILES + t) * 8, 8), 8), :] = value
            far1[pl.ds(pl.multiple_of((b * TILES + t) * 8, 8), 8), :] = jnp.where(
                rows == 6, 1.0, value - centre
            )
            fx, fy, fz = value[0:1], value[1:2], value[2:3]
            fm, fh = value[6:7], value[7:8]
            at = pl.ds(pl.multiple_of(t * 128, 128), 128)
            new = []
            for g in range(W // 16):
                part = pl.ds(g * 16, 16)
                dx = own_wide[0, part, :] - fx
                dy = own_wide[1, part, :] - fy
                dz = own_wide[2, part, :] - fz
                square = jnp.maximum(dx * dx + dy * dy + dz * dz, TINY)
                dist = square * lax.rsqrt(square)
                q = dist * own_wide[4, part, :]
                shell = jnp.maximum(1.0 - q, 0.0)
                shell = shell * shell
                kern = shell * shell * (1.0 + 4.0 * q)
                new.append(acc[g * 16 : g * 16 + 16] + kern * fm)
                inv = 1.0 / (own_wide[3, part, :] + fh)
                shell = jnp.maximum(1.0 - dist * inv, 0.0) * inv
                shell2 = shell * shell
                factor = (shell * (inv * inv)) * shell2
                for k, piece in enumerate(split(factor)):
                    weights[k, b, part, at] = piece
            return jnp.concatenate(new, axis=0)

        acc = lax.fori_loop(0, TILES, tile, jnp.zeros((W, 128), F32))
        sums[pl.ds(b, 1), 0:W] = jnp.sum(jnp.transpose(acc), axis=0, keepdims=True)
        return c

    lax.fori_loop(0, B, density, 0)

    def own_field(ref, k):
        return ref[pl.ds((TILES - 1) * 8 + k, B, stride=TILES * 8), :]

    mass, smooth = own_field(far, 6), own_field(far, 7)
    xi = [own_field(far1, k) for k in range(3)]
    vi = [own_field(far1, 3 + k) for k in range(3)]
    rho = SIGMA / (smooth * smooth * smooth) * sums[...] + (1.0 - live)
    rho = jnp.where(low, rho, 1.0)
    vol = mass / rho
    press = GAMMA_LESS * own_e[0:B] / rho
    rho_ref[...] = rho[:, 0:W]

    def packed(value):
        return jnp.concatenate([value[0:HALF, 0:W], value[HALF:B, 0:W]], axis=1)

    pack_b[0:HALF, :] = packed(vol)
    pack_b[HALF:B, :] = jnp.zeros((HALF, 128), F32)
    b_go()
    reg_b[here] = pack_b[...]

    def store_moment(k, t, value):
        at = pl.ds(pl.multiple_of(t * 128, 128), 128)
        for s, piece in enumerate(split(value)):
            moment[pl.ds(s * 32 + k * 16, 16), at] = piece

    def store_products(t, tile, by):
        store_moment(0, t, jnp.concatenate([tile, tile * by[0:1]], axis=0))
        store_moment(1, t, jnp.concatenate([tile * by[1:2], tile * by[2:3]], axis=0))

    def summed(b, out):
        total = None
        for k in range(SPLITS):
            got = lax.dot_general(
                moment[0 : 32 * (SPLITS - k), :],
                weights[k, b],
                (((1,), (1,)), ((), ())),
                preferred_element_type=F32,
            )
            for s in range(SPLITS - k):
                piece = got[32 * s : 32 * s + 32]
                total = piece if total is None else total + piece
        out[pl.ds(pl.multiple_of(b * 32, 32), 32), 0:W] = total

    def far1_tile(b, t):
        return far1[pl.ds(pl.multiple_of((b * TILES + t) * 8, 8), 8), :]

    def field(ref, k):
        return ref[pl.ds(k, B, stride=32), :]

    def masses(b, c):
        def tile(t, c):
            value = far1_tile(b, t)
            fm = far[pl.ds((b * TILES + t) * 8 + 6, 1), :]
            store_products(t, value * fm, value)
            return c

        lax.fori_loop(0, TILES, tile, 0)
        summed(b, res_m)
        return c

    lax.fori_loop(0, B, masses, 0)

    b_in()

    @pl.when(dom == 0)
    def _():
        for d in range(G):
            reg_b[d] = zero

    @pl.when(dom == D - 1)
    def _():
        for d in range(G):
            reg_b[2 * G + d] = zero

    def tensor(b, c):
        def tile(t, c):
            value = far1_tile(b, t)
            store_products(t, value * joined(1, b, t, load_b), value)
            return c

        lax.fori_loop(0, TILES, tile, 0)
        summed(b, res_l)
        return c

    lax.fori_loop(0, B, tensor, 0)

    s0 = field(res_l, 6)
    s1 = [field(res_l, k) for k in range(3)]
    pairs = ((0, 0), (1, 1), (2, 2), (0, 1), (0, 2), (1, 2))
    corr = []
    for a, b in pairs:
        value = s0 * xi[a] * xi[b] - xi[a] * s1[b] - xi[b] * s1[a] + field(res_l, 8 + 8 * a + b)
        corr.append((2.0 if a == b else 0.0) + SLOPE * value)
    scale = mass * press
    for k in range(6):
        pack = packed(scale * corr[k])
        for p in range(HALF):
            pack_c[p, k : k + 1, :] = pack[p : p + 1]
    for p in range(HALF):
        pack_c[p, 6:8, :] = jnp.zeros((2, 128), F32)
    c_go()
    for p in range(HALF):
        reg_c[here, p] = pack_c[p]

    a0 = field(res_m, 6)
    a1 = [field(res_m, k) for k in range(3)]
    v1 = [field(res_m, 3 + k) for k in range(3)]
    at = ((0, 3, 4), (3, 1, 5), (4, 5, 2))
    grad = [a0 * xi[a] - a1[a] for a in range(3)]
    pull = []
    heat = None
    for a in range(3):
        row = [corr[at[a][b]] for b in range(3)]
        pull.append(press * (row[0] * grad[0] + row[1] * grad[1] + row[2] * grad[2]))
        for b in range(3):
            work = vi[a] * grad[b] - v1[a] * xi[b] + field(res_m, 8 + 8 * b + 3 + a)
            term = row[b] * work
            heat = term if heat is None else heat + term
    energy = own_e[0:B] + STEP_DT * SLOPE * (live * press * heat)

    c_in()

    @pl.when(dom == 0)
    def _():
        for d in range(G):
            for p in range(HALF):
                reg_c[d, p] = zero

    @pl.when(dom == D - 1)
    def _():
        for d in range(G):
            for p in range(HALF):
                reg_c[2 * G + d, p] = zero

    def momentum(b, c):
        def tile(t, c):
            store_products(t, joined(1, b, t, load_c), far1_tile(b, t))
            return c

        lax.fori_loop(0, TILES, tile, 0)
        summed(b, res_q)
        return c

    lax.fori_loop(0, B, momentum, 0)

    for a in range(3):
        far_sum = None
        for b in range(3):
            k = at[a][b]
            term = field(res_q, k) * xi[b] - field(res_q, 8 + 8 * b + k)
            far_sum = term if far_sum is None else far_sum + term
        accel = (-SLOPE) * live * (pull[a] + far_sum)
        velocity = own_field(far, 3 + a) + STEP_DT * accel
        position = own_field(far, a) + STEP_DT * velocity
        out_ref[:, a, :] = position[:, 0:W]
        out_ref[:, 3 + a, :] = velocity[:, 0:W]
    out_ref[:, 6, :] = own_e[B : 2 * B, 0:W]
    out_ref[:, 7, :] = smooth[:, 0:W]
    out_ref[:, 8, :] = energy[:, 0:W]

    meta_out()
    a_out()
    b_out()
    c_out()


def local(sizes, state, counts, neighbours, new_place):
    D, G = sizes
    blocks, _, width = state.shape
    NBR = neighbours.shape[1]
    tiles = (NBR + 2) // 2
    half = blocks // 2
    vmem = pl.BlockSpec(memory_space=pltpu.VMEM)
    smem = pl.BlockSpec(memory_space=pltpu.SMEM)
    sems = pltpu.SemaphoreType.DMA((3 * G,))
    return pl.pallas_call(
        functools.partial(kernel, (D, G, NBR)),
        out_shape=(
            jax.ShapeDtypeStruct(state.shape, F32),
            jax.ShapeDtypeStruct((blocks, width), F32),
        ),
        in_specs=[vmem, vmem, smem, smem],
        out_specs=(vmem, vmem),
        scratch_shapes=[
            pltpu.VMEM((8, 128), jnp.int32),
            pltpu.VMEM((half + 1, 8, 128), F32),
            pltpu.VMEM((8, 128), F32),
            pltpu.VMEM((half, 8, 128), F32),
            pltpu.VMEM((3 * G, 8, 128), jnp.int32),
            pltpu.VMEM((3 * G + 1, half + 1, 8, 128), F32),
            pltpu.VMEM((3 * G + 1, 8, 128), F32),
            pltpu.VMEM((3 * G + 1, half, 8, 128), F32),
            pltpu.VMEM((2, 8, 128), jnp.int32),
            pltpu.SMEM((2, 8, 128), jnp.int32),
            pltpu.VMEM((blocks * tiles * 8, 128), F32),
            pltpu.VMEM((blocks * tiles * 8, 128), F32),
            pltpu.VMEM((5, width, 128), F32),
            pltpu.VMEM((SPLITS, blocks, width, tiles * 128), BF16),
            pltpu.VMEM((16, 128), F32),
            pltpu.VMEM((8, 128), F32),
            pltpu.VMEM((blocks * 32, 128), F32),
            pltpu.VMEM((blocks * 32, 128), F32),
            pltpu.VMEM((blocks * 32, 128), F32),
            pltpu.VMEM((SPLITS * 32, tiles * 128), BF16),
            pltpu.SemaphoreType.DMA,
        ]
        + [sems] * 8,
        compiler_params=pltpu.CompilerParams(
            collective_id=0, has_side_effects=True, vmem_limit_bytes=40 * 2**20
        ),
    )(state, neighbours, counts, new_place)


def solution(mesh):
    sizes = (mesh.shape["dom"], mesh.shape["seg"])
    both = ("dom", "seg")
    return jax.shard_map(
        functools.partial(local, sizes),
        mesh=mesh,
        in_specs=(P(both, None, None), P(both), P(both, None), P(both)),
        out_specs=(P(both, None, None), P(both, None)),
        check_vma=False,
    )
```

time: 345 us -> 88.2 us (0.26); the launches traced: 338 us -> 87.5 us
  blocking collectives: 125 us -> 0 us
  Pallas kernels: 0 us -> 84.8 us
  local copies, waits for them, and re-layouts: 61.7 us -> 2.03 us
  starting transfers between devices: 56.4 us -> 0 us
  loops' own time: 53 us -> 0 us
  other arithmetic: 38.6 us -> 0 us
    all_gather x5 -> x0, blocking collectives: 112 us -> none  [the longest x3 67.3 us: spread(): whole = lax.all_gather(values, 'seg', axis=0, tiled=True)]
    pallas_call x0 -> x1, Pallas kernels: none -> 84.8 us  [local(): pl.pallas_call(functools.partial(kernel, (D, G, NBR)), out_shape=(jax.Sha...]
    ppermute x6 -> x0, starting transfers between devices: 56.4 us -> none  [the longest x3 50.6 us: with_halo(): lax.ppermute(lax.slice_in_dim(block, 0, width, axis=dim), axis, backward)]
    another operation x3 -> x0, loops' own time: 53 us -> none  [the longest x1 18.2 us: local(): accel, heat = lax.map(third, block_ids)]
    gather x42 -> x0, local copies, waits for them, and re-layouts: 24.3 us -> none  [the longest x40 23.2 us: tile_of(): tile = jnp.take(region, index, axis=0)]
    reduce_sum x49 -> x0, other arithmetic: 18.6 us -> none  [the longest x8 6.64 us: tensor_tile(): jnp.sum(weight * diff[a] * diff[b], axis=1)]
    dynamic_slice x24 -> x0, local copies, waits for them, and re-layouts: 16 us -> none  [local(): rho = lax.map(first, block_ids) + (1.0 - live)]
    unnamed x1 -> x0, blocking collectives: 12.7 us -> none
  transfers between devices with their start and end apart: 6 -> 0, of which waited for: 1 -> 0; matrix products, arithmetic and copies ran while one was open for 2% -> 0% of each run, Pallas kernels for 0% -> 0%
where the time goes in v1:
time: 88.2 us; the launch traced here: 87.5 us
  Pallas kernels  84.8 us (96%)
  local copies, waits for them, and re-layouts  2.03 us (2%)
    pallas_call x1, Pallas kernels, local(): pl.pallas_call(functools.partial(kernel, (D, G, NBR)), out_shape=(jax.Sha...  84.8 us

profile of v1, /device:TPU:1, one launch (start us, length us, event | category | flops | bytes accessed | tf_op | source)
XLA Modules:
  0.0 87.5 jit_solution(9667917949549283284)
XLA Ops:
  0.6 0.0 copy-start.2
  0.6 0.0 copy-start
  0.7 0.0 copy-start.1
  0.7 0.8 copy.6.state_ref
  1.5 0.0 copy-done.2
  1.5 0.0 copy-done
  1.5 0.0 copy-done.1
  1.5 84.8 %shard_map.59 = (f32[8,9,64]{2,1,0:T(8,128)S(1)}, f32[8,64]{1,0:T(8,128)S(1)}) custom-call(f32[8,9,64]{2,1,0:T(8,128)S(1)} %copy.6.state_ref, s32[8,26]{1,0:T(8,128)S(1)} %copy-done, s32[8]{0:T(128)S(1)} %copy-done.1, s32[8]{0:T(128)S(1)} %copy-done.2), custom_call_target="tpu_custom_call" | custom-call | tf_op jit(solution)/shard_map/pallas_call | solution.py:487
  86.3 0.6 copy.7
  86.9 0.6 copy.9
Async XLA Ops:
  0.6 0.8 copy-start.2
  0.6 0.8 copy-start
  0.7 0.8 copy-start.1

commit v2 on v1

--- a/solution.py
+++ b/solution.py
@@ -50,6 +50,8 @@
     far,
     far1,
     own_wide,
+    smooth_wide,
+    dists,
     weights,
     own_e,
     sums,
@@ -77,8 +79,11 @@
     dom = lax.axis_index("dom")
     seg = lax.axis_index("seg")
 
+    def wrapped(value, size):
+        return value & (size - 1) if size & (size - 1) == 0 else lax.rem(value, size)
+
     def target(delta, o):
-        return (lax.rem(dom + delta + D, D), lax.rem(seg + o, G))
+        return (wrapped(dom + delta + D, D), wrapped(seg + o, G))
 
     def each_peer(action):
         for delta in (-1, 1):
@@ -87,13 +92,13 @@
                 action(delta, o)
                 return c
 
-            lax.fori_loop(0, G, outer, 0)
+            lax.fori_loop(0, G, outer, 0, unroll=True)
 
         def inner(o, c):
             action(0, o)
             return c
 
-        lax.fori_loop(1, G, inner, 0)
+        lax.fori_loop(1, G, inner, 0, unroll=True)
 
     barrier = pltpu.get_barrier_semaphore()
 
@@ -116,14 +121,14 @@
     meta[...] = note
     meta[:, 0:NBR] = nb_ref[...]
     for p in range(HALF):
-        pair = jnp.concatenate([state_ref[p, 0:8, :], state_ref[p + HALF, 0:8, :]], axis=1)
+        pair = jnp.concatenate(
+            [state_ref[pl.ds(q, 8, stride=B), :] for q in (p, p + HALF)], axis=1
+        )
         limit = jnp.where(low, counts_ref[p], counts_ref[p + HALF] + W)
         pack_a[p] = jnp.where((rows == 6) & (lanes >= limit), 0.0, pair)
-        pack_a[HALF, p : p + 1] = jnp.concatenate(
-            [state_ref[p, 8:9, :], state_ref[p + HALF, 8:9, :]], axis=1
-        )
-        pack_a[HALF, p + HALF : p + HALF + 1] = jnp.concatenate(
-            [state_ref[p, 6:7, :], state_ref[p + HALF, 6:7, :]], axis=1
+    for k, f in enumerate((8, 6)):
+        pack_a[HALF, k * HALF : k * HALF + HALF] = jnp.concatenate(
+            [state_ref[f * B + h * HALF : f * B + h * HALF + HALF, :] for h in (0, 1)], axis=1
         )
 
     pl.semaphore_wait(barrier, 3 * G - 1)
@@ -141,7 +146,7 @@
             )
 
         def take(delta, o):
-            slot = (1 + delta) * G + lax.rem(seg + o, G)
+            slot = (1 + delta) * G + wrapped(seg + o, G)
             return pltpu.make_async_remote_copy(
                 src_ref=src(delta),
                 dst_ref=dst(slot, delta),
@@ -271,7 +276,8 @@
         turned = jnp.transpose(own)[0:W]
         for k, field in enumerate((0, 1, 2, 7)):
             own_wide[k] = jnp.broadcast_to(turned[:, field : field + 1], (W, 128))
-        own_wide[4] = 0.5 / own_wide[3]
+        smooth_wide[b] = own_wide[3]
+        own_wide[3] = 0.5 / own_wide[3]
 
         def tile(t, acc):
             value = joined(0, b, t, load_a)
@@ -280,7 +286,7 @@
                 rows == 6, 1.0, value - centre
             )
             fx, fy, fz = value[0:1], value[1:2], value[2:3]
-            fm, fh = value[6:7], value[7:8]
+            fm = value[6:7]
             at = pl.ds(pl.multiple_of(t * 128, 128), 128)
             new = []
             for g in range(W // 16):
@@ -290,20 +296,15 @@
                 dz = own_wide[2, part, :] - fz
                 square = jnp.maximum(dx * dx + dy * dy + dz * dz, TINY)
                 dist = square * lax.rsqrt(square)
-                q = dist * own_wide[4, part, :]
+                q = dist * own_wide[3, part, :]
                 shell = jnp.maximum(1.0 - q, 0.0)
                 shell = shell * shell
                 kern = shell * shell * (1.0 + 4.0 * q)
                 new.append(acc[g * 16 : g * 16 + 16] + kern * fm)
-                inv = 1.0 / (own_wide[3, part, :] + fh)
-                shell = jnp.maximum(1.0 - dist * inv, 0.0) * inv
-                shell2 = shell * shell
-                factor = (shell * (inv * inv)) * shell2
-                for k, piece in enumerate(split(factor)):
-                    weights[k, b, part, at] = piece
+                dists[b, part, at] = dist
             return jnp.concatenate(new, axis=0)
 
-        acc = lax.fori_loop(0, TILES, tile, jnp.zeros((W, 128), F32))
+        acc = lax.fori_loop(0, TILES, tile, jnp.zeros((W, 128), F32), unroll=TILES)
         sums[pl.ds(b, 1), 0:W] = jnp.sum(jnp.transpose(acc), axis=0, keepdims=True)
         return c
 
@@ -329,20 +330,28 @@
     b_go()
     reg_b[here] = pack_b[...]
 
-    def store_moment(k, t, value):
+    def blocks_of(body):
+        def several(i, c):
+            for k in range(4):
+                body(i * 4 + k, k)
+            return c
+
+        lax.fori_loop(0, B // 4, several, 0)
+
+    def store_moment(k, t, value, way):
         at = pl.ds(pl.multiple_of(t * 128, 128), 128)
         for s, piece in enumerate(split(value)):
-            moment[pl.ds(s * 32 + k * 16, 16), at] = piece
-
-    def store_products(t, tile, by):
-        store_moment(0, t, jnp.concatenate([tile, tile * by[0:1]], axis=0))
-        store_moment(1, t, jnp.concatenate([tile * by[1:2], tile * by[2:3]], axis=0))
-
-    def summed(b, out):
+            moment[way, pl.ds(s * 32 + k * 16, 16), at] = piece
+
+    def store_products(t, tile, by, way):
+        store_moment(0, t, jnp.concatenate([tile, tile * by[0:1]], axis=0), way)
+        store_moment(1, t, jnp.concatenate([tile * by[1:2], tile * by[2:3]], axis=0), way)
+
+    def summed(b, out, way):
         total = None
         for k in range(SPLITS):
             got = lax.dot_general(
-                moment[0 : 32 * (SPLITS - k), :],
+                moment[way, 0 : 32 * (SPLITS - k), :],
                 weights[k, b],
                 (((1,), (1,)), ((), ())),
                 preferred_element_type=F32,
@@ -358,42 +367,47 @@
     def field(ref, k):
         return ref[pl.ds(k, B, stride=32), :]
 
-    def masses(b, c):
+    def slopes(b, c):
+        def tile(t, c):
+            fh = far[pl.ds((b * TILES + t) * 8 + 7, 1), :]
+            at = pl.ds(pl.multiple_of(t * 128, 128), 128)
+            for g in range(W // 16):
+                part = pl.ds(g * 16, 16)
+                inv = 1.0 / (smooth_wide[b, part, :] + fh)
+                shell = jnp.maximum(1.0 - dists[b, part, at] * inv, 0.0) * inv
+                shell2 = shell * shell
+                factor = (shell * (inv * inv)) * shell2
+                for k, piece in enumerate(split(factor)):
+                    weights[k, b, part, at] = piece
+            return c
+
+        lax.fori_loop(0, TILES, tile, 0, unroll=TILES)
+        return c
+
+    lax.fori_loop(0, B, slopes, 0)
+
+    b_in()
+
+    @pl.when(dom == 0)
+    def _():
+        for d in range(G):
+            reg_b[d] = zero
+
+    @pl.when(dom == D - 1)
+    def _():
+        for d in range(G):
+            reg_b[2 * G + d] = zero
+
+    def tensor(b, way):
         def tile(t, c):
             value = far1_tile(b, t)
-            fm = far[pl.ds((b * TILES + t) * 8 + 6, 1), :]
-            store_products(t, value * fm, value)
+            store_products(t, value * joined(1, b, t, load_b), value, way)
             return c
 
-        lax.fori_loop(0, TILES, tile, 0)
-        summed(b, res_m)
-        return c
-
-    lax.fori_loop(0, B, masses, 0)
-
-    b_in()
-
-    @pl.when(dom == 0)
-    def _():
-        for d in range(G):
-            reg_b[d] = zero
-
-    @pl.when(dom == D - 1)
-    def _():
-        for d in range(G):
-            reg_b[2 * G + d] = zero
-
-    def tensor(b, c):
-        def tile(t, c):
-            value = far1_tile(b, t)
-            store_products(t, value * joined(1, b, t, load_b), value)
-            return c
-
-        lax.fori_loop(0, TILES, tile, 0)
-        summed(b, res_l)
-        return c
-
-    lax.fori_loop(0, B, tensor, 0)
+        lax.fori_loop(0, TILES, tile, 0, unroll=TILES)
+        summed(b, res_l, way)
+
+    blocks_of(tensor)
 
     s0 = field(res_l, 6)
     s1 = [field(res_l, k) for k in range(3)]
@@ -413,6 +427,18 @@
     for p in range(HALF):
         reg_c[here, p] = pack_c[p]
 
+    def masses(b, way):
+        def tile(t, c):
+            value = far1_tile(b, t)
+            fm = far[pl.ds((b * TILES + t) * 8 + 6, 1), :]
+            store_products(t, value * fm, value, way)
+            return c
+
+        lax.fori_loop(0, TILES, tile, 0, unroll=TILES)
+        summed(b, res_m, way)
+
+    blocks_of(masses)
+
     a0 = field(res_m, 6)
     a1 = [field(res_m, k) for k in range(3)]
     v1 = [field(res_m, 3 + k) for k in range(3)]
@@ -443,16 +469,15 @@
             for p in range(HALF):
                 reg_c[2 * G + d, p] = zero
 
-    def momentum(b, c):
+    def momentum(b, way):
         def tile(t, c):
-            store_products(t, joined(1, b, t, load_c), far1_tile(b, t))
+            store_products(t, joined(1, b, t, load_c), far1_tile(b, t), way)
             return c
 
-        lax.fori_loop(0, TILES, tile, 0)
-        summed(b, res_q)
-        return c
-
-    lax.fori_loop(0, B, momentum, 0)
+        lax.fori_loop(0, TILES, tile, 0, unroll=TILES)
+        summed(b, res_q, way)
+
+    blocks_of(momentum)
 
     for a in range(3):
         far_sum = None
@@ -463,11 +488,11 @@
         accel = (-SLOPE) * live * (pull[a] + far_sum)
         velocity = own_field(far, 3 + a) + STEP_DT * accel
         position = own_field(far, a) + STEP_DT * velocity
-        out_ref[:, a, :] = position[:, 0:W]
-        out_ref[:, 3 + a, :] = velocity[:, 0:W]
-    out_ref[:, 6, :] = own_e[B : 2 * B, 0:W]
-    out_ref[:, 7, :] = smooth[:, 0:W]
-    out_ref[:, 8, :] = energy[:, 0:W]
+        out_ref[pl.ds((a) * B, B), :] = position[:, 0:W]
+        out_ref[pl.ds((3 + a) * B, B), :] = velocity[:, 0:W]
+    out_ref[pl.ds((6) * B, B), :] = own_e[B : 2 * B, 0:W]
+    out_ref[pl.ds((7) * B, B), :] = smooth[:, 0:W]
+    out_ref[pl.ds((8) * B, B), :] = energy[:, 0:W]
 
     meta_out()
     a_out()
@@ -484,10 +509,10 @@
     vmem = pl.BlockSpec(memory_space=pltpu.VMEM)
     smem = pl.BlockSpec(memory_space=pltpu.SMEM)
     sems = pltpu.SemaphoreType.DMA((3 * G,))
-    return pl.pallas_call(
+    moved, rho = pl.pallas_call(
         functools.partial(kernel, (D, G, NBR)),
         out_shape=(
-            jax.ShapeDtypeStruct(state.shape, F32),
+            jax.ShapeDtypeStruct((9 * blocks, width), F32),
             jax.ShapeDtypeStruct((blocks, width), F32),
         ),
         in_specs=[vmem, vmem, smem, smem],
@@ -505,21 +530,29 @@
             pltpu.SMEM((2, 8, 128), jnp.int32),
             pltpu.VMEM((blocks * tiles * 8, 128), F32),
             pltpu.VMEM((blocks * tiles * 8, 128), F32),
-            pltpu.VMEM((5, width, 128), F32),
+            pltpu.VMEM((4, width, 128), F32),
+            pltpu.VMEM((blocks, width, 128), F32),
+            pltpu.VMEM((blocks, width, tiles * 128), F32),
             pltpu.VMEM((SPLITS, blocks, width, tiles * 128), BF16),
             pltpu.VMEM((16, 128), F32),
             pltpu.VMEM((8, 128), F32),
             pltpu.VMEM((blocks * 32, 128), F32),
             pltpu.VMEM((blocks * 32, 128), F32),
             pltpu.VMEM((blocks * 32, 128), F32),
-            pltpu.VMEM((SPLITS * 32, tiles * 128), BF16),
+            pltpu.VMEM((4, SPLITS * 32, tiles * 128), BF16),
             pltpu.SemaphoreType.DMA,
         ]
         + [sems] * 8,
         compiler_params=pltpu.CompilerParams(
             collective_id=0, has_side_effects=True, vmem_limit_bytes=40 * 2**20
         ),
-    )(state, neighbours, counts, new_place)
+    )(
+        jnp.transpose(state, (1, 0, 2)).reshape(9 * blocks, width),
+        neighbours,
+        counts,
+        new_place,
+    )
+    return (jnp.transpose(moved.reshape(9, blocks, width), (1, 0, 2)), rho)
 
 
 def solution(mesh):

time: 88.2 us -> 56.7 us (0.64)
  Pallas kernels: 84.8 us -> 52.5 us
  local copies, waits for them, and re-layouts: 2.03 us -> 3.32 us
    pallas_call x1, Pallas kernels: 84.8 us -> 52.5 us  [local(): pl.pallas_call(functools.partial(kernel, (D, G, NBR)), out_shape=(jax.Sha...]
    unnamed x8 -> x10, local copies, waits for them, and re-layouts: 1.4 us -> 3.32 us
where the time goes in v2:
time: 56.7 us; the launch traced here: 56.4 us
  Pallas kernels  52.5 us (93%)
  local copies, waits for them, and re-layouts  3.32 us (6%)
  between operations  0.66 us (1%)
    pallas_call x1, Pallas kernels, local(): pl.pallas_call(functools.partial(kernel, (D, G, NBR)), out_shape=(jax.Sha...  52.5 us
    unnamed x10, local copies, waits for them, and re-layouts  3.32 us

profile of v2, /device:TPU:1, one launch (start us, length us, event | category | flops | bytes accessed | tf_op | source)
XLA Modules:
  0.0 56.4 jit_solution(6664290197059511231)
XLA Ops:
  0.6 0.0 copy-start.3
  0.6 0.0 copy-start.2
  0.7 0.6 %copy-done.3 = s32[8]{0:T(128)S(1)} copy-done((s32[8]{0:T(128)S(1)}, s32[8]{0:T(128)}, u32[]{:S(2)}) %copy-start.3) | copy-done | bytes 56
  1.3 0.0 copy-done.2
  1.3 0.0 copy-start
  1.3 0.8 %copy-done = f32[8,9,64]{2,0,1:T(8,128)S(1)} copy-done((f32[8,9,64]{2,0,1:T(8,128)S(1)}, f32[8,9,64]{2,0,1:T(8,128)}, u32[]{:S(2)}) %copy-start) | copy-done | bytes 18456
  2.1 0.0 copy-start.1
  2.1 0.7 %copy-done.1 = s32[8,26]{1,0:T(8,128)S(1)} copy-done((s32[8,26]{1,0:T(8,128)S(1)}, s32[8,26]{1,0:T(8,128)}, u32[]{:S(2)}) %copy-start.1) | copy-done | bytes 856
  2.8 52.5 %shard_map.59 = (f32[72,64]{1,0:T(8,128)S(1)}, f32[8,64]{1,0:T(8,128)S(1)}) custom-call(f32[72,64]{1,0:T(8,128)S(1)} %bitcast.6, s32[8,26]{1,0:T(8,128)S(1)} %copy-done.1, s32[8]{0:T(128)S(1)} %copy-done.2, s32[8]{0:T(128)S(1)} %copy-done.3), custom_call_target="tpu_custom_call" | custom-call | tf_op jit(solution)/shard_map/pallas_call | solution.py:512
  55.2 0.6 %copy.8 = f32[8,9,64]{2,0,1:T(8,128)} copy(f32[8,9,64]{2,0,1:T(8,128)S(1)} %bitcast.7) | data formatting | bytes 36864
  55.8 0.6 %copy.9 = f32[8,64]{1,0:T(8,128)} copy(f32[8,64]{1,0:T(8,128)S(1)} %get-tuple-element.9) | data formatting | bytes 4096
Async XLA Ops:
  0.6 0.7 %copy-start.3 = (s32[8]{0:T(128)S(1)}, s32[8]{0:T(128)}, u32[]{:S(2)}) copy-start(s32[8]{0:T(128)} %place_ref.1) | copy-start | bytes 100
  0.6 0.7 %copy-start.2 = (s32[8]{0:T(128)S(1)}, s32[8]{0:T(128)}, u32[]{:S(2)}) copy-start(s32[8]{0:T(128)} %counts_ref.1) | copy-start | bytes 100
  1.3 0.8 %copy-start = (f32[8,9,64]{2,0,1:T(8,128)S(1)}, f32[8,9,64]{2,0,1:T(8,128)}, u32[]{:S(2)}) copy-start(f32[8,9,64]{2,0,1:T(8,128)} %param.4) | copy-start | bytes 55300
  2.1 0.7 %copy-start.1 = (s32[8,26]{1,0:T(8,128)S(1)}, s32[8,26]{1,0:T(8,128)}, u32[]{:S(2)}) copy-start(s32[8,26]{1,0:T(8,128)} %nb_ref.1) | copy-start | bytes 2500

commit v3 on v2

--- a/solution.py
+++ b/solution.py
@@ -31,10 +31,10 @@
 
 def kernel(
     dims,
-    state_ref,
-    nb_ref,
-    counts_ref,
-    place_ref,
+    state_hbm,
+    nb_hbm,
+    counts_hbm,
+    place_hbm,
     out_ref,
     rho_ref,
     meta,
@@ -50,6 +50,8 @@
     far,
     far1,
     own_wide,
+    centres,
+    accs,
     smooth_wide,
     dists,
     weights,
@@ -59,6 +61,11 @@
     res_m,
     res_q,
     moment,
+    state_ref,
+    nb_ref,
+    counts_ref,
+    place_ref,
+    fetch_sem,
     copy_sem,
     send_m,
     recv_m,
@@ -85,20 +92,23 @@
     def target(delta, o):
         return (wrapped(dom + delta + D, D), wrapped(seg + o, G))
 
+    steps = (6, 2, 5, 7, 4, 1, 3, 0) if G == 8 else tuple(range(G))
+    away = 2 * (dom & 1) - 1
+
+    def others(action):
+        for o in steps:
+            action(away, o)
+        for o in steps:
+            action(-away, o)
+
+    def group(action):
+        for o in steps:
+            if o:
+                action(0, o)
+
     def each_peer(action):
-        for delta in (-1, 1):
-
-            def outer(o, c, delta=delta):
-                action(delta, o)
-                return c
-
-            lax.fori_loop(0, G, outer, 0, unroll=True)
-
-        def inner(o, c):
-            action(0, o)
-            return c
-
-        lax.fori_loop(1, G, inner, 0, unroll=True)
+        others(action)
+        group(action)
 
     barrier = pltpu.get_barrier_semaphore()
 
@@ -106,6 +116,21 @@
         pl.semaphore_signal(barrier, inc=1, device_id=target(delta, o), device_id_type=MESH)
 
     each_peer(greet)
+    fetches = [
+        pltpu.make_async_copy(src, dst, fetch_sem.at[k])
+        for k, (src, dst) in enumerate(
+            (
+                (place_hbm, place_ref),
+                (counts_hbm, counts_ref),
+                (nb_hbm, nb_ref),
+                (state_hbm, state_ref),
+            )
+        )
+    ]
+    for fetch in fetches:
+        fetch.start()
+    for fetch in fetches:
+        fetch.wait()
 
     rows = lax.broadcasted_iota(jnp.int32, (B, 128), 0)
     lanes = lax.broadcasted_iota(jnp.int32, (B, 128), 1)
@@ -133,7 +158,7 @@
 
     pl.semaphore_wait(barrier, 3 * G - 1)
 
-    def sent(src, dst, send_sem, recv_sem):
+    def sent(src, dst, send_sem, recv_sem, each_peer=each_peer):
         def make(delta, o):
             slot = (1 - delta) * G + seg
             return pltpu.make_async_remote_copy(
@@ -162,20 +187,26 @@
             lambda: each_peer(lambda delta, o: make(delta, o).wait_send()),
         )
 
-    meta_go, meta_in, meta_out = sent(
-        lambda d: meta, lambda s, d: reg_m.at[s], send_m, recv_m
+    near_go, near_in, near_out = sent(
+        lambda d: meta, lambda s, d: reg_m.at[s], send_m, recv_m, group
+    )
+    wide_go, wide_in, wide_out = sent(
+        lambda d: meta, lambda s, d: reg_m.at[s], send_m, recv_m, others
     )
     a_go, a_in, a_out = sent(
-        lambda d: pack_a if d == 0 else pack_a.at[0:HALF],
-        lambda s, d: reg_a.at[s] if d == 0 else reg_a.at[s, 0:HALF],
+        lambda d: pack_a if type(d) is int else pack_a.at[0:HALF],
+        lambda s, d: reg_a.at[s] if type(d) is int else reg_a.at[s, 0:HALF],
         send_a,
         recv_a,
     )
     b_go, b_in, b_out = sent(lambda d: pack_b, lambda s, d: reg_b.at[s], send_b, recv_b)
-    c_go, c_in, c_out = sent(lambda d: pack_c, lambda s, d: reg_c.at[s], send_c, recv_c)
-
-    meta_go()
+    c_go, c_in, c_out = sent(
+        lambda d: pack_c.at[:, 0:6], lambda s, d: reg_c.at[s, :, 0:6], send_c, recv_c
+    )
+
+    near_go()
     a_go()
+    wide_go()
 
     here = G + seg
     reg_m[here] = meta[...]
@@ -188,7 +219,7 @@
         reg_c[none, p] = zero
     reg_a[none, HALF] = zero
 
-    meta_in()
+    near_in()
     lists = jnp.zeros((B, 128), jnp.int32)
     notes = [reg_m[G + d] for d in range(G)]
     places = [jnp.broadcast_to(note[:, PLACE : PLACE + 1], (B, 128)) for note in notes]
@@ -199,6 +230,120 @@
         for shift in (4, 2, 1):
             found = found + pltpu.roll(found, shift, 0)
         lists = jnp.where(rows == b, found, lists)
+    inside = jnp.clip(lists, 0, 3 * SLAB)
+    half = (inside >> 2) & 1
+    table[0] = (((inside >> 3) * (HALF + 1) + (inside & 3)) << 1) | half
+    live = jnp.where(lanes < jnp.broadcast_to(lists[:, COUNT : COUNT + 1], (B, 128)), 1.0, 0.0)
+
+    def to_smem(which):
+        return pltpu.make_async_copy(table.at[which], table_smem.at[which], copy_sem)
+
+    to_smem(0).start()
+    to_smem(0).wait()
+
+    a_in()
+
+    @pl.when(dom == 0)
+    def _():
+        for d in range(G):
+            for p in range(HALF):
+                reg_a[d, p] = zero
+
+    @pl.when(dom == D - 1)
+    def _():
+        for d in range(G):
+            for p in range(HALF):
+                reg_a[2 * G + d, p] = zero
+
+    def joined(which, b, t, load):
+        even, odd = table_smem[which, b, 2 * t], table_smem[which, b, 2 * t + 1]
+        left, right = load(even >> 1), load(odd >> 1)
+        left = pltpu.roll(left, (even & 1) * W, 1)
+        right = pltpu.roll(right, W - (odd & 1) * W, 1)
+        mask = low if left.shape[0] == B else low[0:1]
+        return jnp.where(mask, left, right)
+
+    def load_a(tile):
+        return reg_a[lax.div(tile, HALF + 1), lax.rem(tile, HALF + 1)]
+
+    def load_b(row):
+        return reg_b[row >> 2, pl.ds(row & 3, 1), :]
+
+    def load_c(tile):
+        return reg_c[tile >> 2, tile & 3]
+
+    for b in range(B):
+        own = joined(0, b, TILES - 1, load_a)
+        where_own = table_smem[0, b, SELF]
+        dev, pair = lax.div(where_own >> 1, HALF + 1), lax.rem(where_own >> 1, HALF + 1)
+        shift = (where_own & 1) * W
+        own_e[b : b + 1, :] = pltpu.roll(reg_a[dev, HALF, pl.ds(pair, 1), :], shift, 1)
+        own_e[B + b : B + b + 1, :] = pltpu.roll(
+            reg_a[dev, HALF, pl.ds(HALF + pair, 1), :], shift, 1
+        )
+        centre = jnp.sum(jnp.where(low, own, 0.0), axis=1, keepdims=True) * (1.0 / W)
+        centre = jnp.where(rows < 6, jnp.broadcast_to(centre, (B, 128)), 0.0)
+        centres[b] = centre
+        turned = jnp.transpose(own)[0:W]
+        for k, field in enumerate((0, 1, 2, 7)):
+            own_wide[b, k] = jnp.broadcast_to(turned[:, field : field + 1], (W, 128))
+        smooth_wide[b] = own_wide[b, 3]
+        own_wide[b, 3] = 0.5 / own_wide[b, 3]
+
+    def density(b, c):
+        centre = centres[b]
+
+        def tile(t, acc):
+            value = joined(0, b, t, load_a)
+            far[pl.ds(pl.multiple_of((b * TILES + t) * 8, 8), 8), :] = value
+            far1[pl.ds(pl.multiple_of((b * TILES + t) * 8, 8), 8), :] = jnp.where(
+                rows == 6, 1.0, value - centre
+            )
+            fx, fy, fz = value[0:1], value[1:2], value[2:3]
+            fm = value[6:7]
+            at = pl.ds(pl.multiple_of(t * 128, 128), 128)
+            new = []
+            for g in range(W // 16):
+                part = pl.ds(g * 16, 16)
+                dx = own_wide[b, 0, part, :] - fx
+                dy = own_wide[b, 1, part, :] - fy
+                dz = own_wide[b, 2, part, :] - fz
+                square = jnp.maximum(dx * dx + dy * dy + dz * dz, TINY)
+                dist = square * lax.rsqrt(square)
+                q = dist * own_wide[b, 3, part, :]
+                shell = jnp.maximum(1.0 - q, 0.0)
+                shell = shell * shell
+                kern = shell * shell * (1.0 + 4.0 * q)
+                new.append(acc[g * 16 : g * 16 + 16] + kern * fm)
+                dists[b, part, at] = dist
+            return jnp.concatenate(new, axis=0)
+
+        accs[b] = lax.fori_loop(0, TILES, tile, jnp.zeros((W, 128), F32), unroll=TILES)
+        return c
+
+    lax.fori_loop(0, B, density, 0)
+    for b in range(B):
+        sums[b : b + 1, 0:W] = jnp.sum(jnp.transpose(accs[b]), axis=0, keepdims=True)
+
+    def own_field(ref, k):
+        return ref[pl.ds((TILES - 1) * 8 + k, B, stride=TILES * 8), :]
+
+    mass, smooth = own_field(far, 6), own_field(far, 7)
+    xi = [own_field(far1, k) for k in range(3)]
+    vi = [own_field(far1, 3 + k) for k in range(3)]
+    rho = SIGMA / (smooth * smooth * smooth) * sums[...] + (1.0 - live)
+    rho = jnp.where(low, rho, 1.0)
+    vol = mass / rho
+    press = GAMMA_LESS * own_e[0:B] / rho
+    rho_ref[...] = rho[:, 0:W]
+
+    def packed(value):
+        return jnp.concatenate([value[0:HALF, 0:W], value[HALF:B, 0:W]], axis=1)
+
+    pack_b[0:HALF, :] = packed(vol)
+    pack_b[HALF:B, :] = jnp.zeros((HALF, 128), F32)
+    b_go()
+    wide_in()
     spread = []
     for q in range(3):
         total = reg_m[q * G, 0:1, :]
@@ -221,113 +366,10 @@
         for q in range(3):
             got = jnp.take_along_axis(spread[q], inside, axis=1, mode="promise_in_bounds")
             moved = jnp.where((lists >= q * SLAB) & (lists < (q + 1) * SLAB), q * SLAB + got, moved)
-    inside = jnp.clip(lists, 0, 3 * SLAB)
     moved = jnp.clip(moved, 0, 3 * SLAB)
-    half = (inside >> 2) & 1
-    table[0] = (((inside >> 3) * (HALF + 1) + (inside & 3)) << 1) | half
     table[1] = (((moved >> 3) * HALF + (moved & 3)) << 1) | ((moved >> 2) & 1)
-    live = jnp.where(lanes < jnp.broadcast_to(lists[:, COUNT : COUNT + 1], (B, 128)), 1.0, 0.0)
-    to_smem = pltpu.make_async_copy(table, table_smem, copy_sem)
-    to_smem.start()
-    to_smem.wait()
-
-    a_in()
-
-    @pl.when(dom == 0)
-    def _():
-        for d in range(G):
-            for p in range(HALF):
-                reg_a[d, p] = zero
-
-    @pl.when(dom == D - 1)
-    def _():
-        for d in range(G):
-            for p in range(HALF):
-                reg_a[2 * G + d, p] = zero
-
-    def joined(which, b, t, load):
-        even, odd = table_smem[which, b, 2 * t], table_smem[which, b, 2 * t + 1]
-        left, right = load(even >> 1), load(odd >> 1)
-        left = pltpu.roll(left, (even & 1) * W, 1)
-        right = pltpu.roll(right, W - (odd & 1) * W, 1)
-        mask = low if left.shape[0] == B else low[0:1]
-        return jnp.where(mask, left, right)
-
-    def load_a(tile):
-        return reg_a[lax.div(tile, HALF + 1), lax.rem(tile, HALF + 1)]
-
-    def load_b(row):
-        return reg_b[row >> 2, pl.ds(row & 3, 1), :]
-
-    def load_c(tile):
-        return reg_c[tile >> 2, tile & 3]
-
-    def density(b, c):
-        own = joined(0, b, TILES - 1, load_a)
-        where_own = table_smem[0, b, SELF]
-        dev, pair = lax.div(where_own >> 1, HALF + 1), lax.rem(where_own >> 1, HALF + 1)
-        shift = (where_own & 1) * W
-        own_e[pl.ds(b, 1), :] = pltpu.roll(reg_a[dev, HALF, pl.ds(pair, 1), :], shift, 1)
-        own_e[pl.ds(B + b, 1), :] = pltpu.roll(
-            reg_a[dev, HALF, pl.ds(HALF + pair, 1), :], shift, 1
-        )
-        centre = jnp.sum(jnp.where(low, own, 0.0), axis=1, keepdims=True) * (1.0 / W)
-        centre = jnp.where(rows < 6, jnp.broadcast_to(centre, (B, 128)), 0.0)
-        turned = jnp.transpose(own)[0:W]
-        for k, field in enumerate((0, 1, 2, 7)):
-            own_wide[k] = jnp.broadcast_to(turned[:, field : field + 1], (W, 128))
-        smooth_wide[b] = own_wide[3]
-        own_wide[3] = 0.5 / own_wide[3]
-
-        def tile(t, acc):
-            value = joined(0, b, t, load_a)
-            far[pl.ds(pl.multiple_of((b * TILES + t) * 8, 8), 8), :] = value
-            far1[pl.ds(pl.multiple_of((b * TILES + t) * 8, 8), 8), :] = jnp.where(
-                rows == 6, 1.0, value - centre
-            )
-            fx, fy, fz = value[0:1], value[1:2], value[2:3]
-            fm = value[6:7]
-            at = pl.ds(pl.multiple_of(t * 128, 128), 128)
-            new = []
-            for g in range(W // 16):
-                part = pl.ds(g * 16, 16)
-                dx = own_wide[0, part, :] - fx
-                dy = own_wide[1, part, :] - fy
-                dz = own_wide[2, part, :] - fz
-                square = jnp.maximum(dx * dx + dy * dy + dz * dz, TINY)
-                dist = square * lax.rsqrt(square)
-                q = dist * own_wide[3, part, :]
-                shell = jnp.maximum(1.0 - q, 0.0)
-                shell = shell * shell
-                kern = shell * shell * (1.0 + 4.0 * q)
-                new.append(acc[g * 16 : g * 16 + 16] + kern * fm)
-                dists[b, part, at] = dist
-            return jnp.concatenate(new, axis=0)
-
-        acc = lax.fori_loop(0, TILES, tile, jnp.zeros((W, 128), F32), unroll=TILES)
-        sums[pl.ds(b, 1), 0:W] = jnp.sum(jnp.transpose(acc), axis=0, keepdims=True)
-        return c
-
-    lax.fori_loop(0, B, density, 0)
-
-    def own_field(ref, k):
-        return ref[pl.ds((TILES - 1) * 8 + k, B, stride=TILES * 8), :]
-
-    mass, smooth = own_field(far, 6), own_field(far, 7)
-    xi = [own_field(far1, k) for k in range(3)]
-    vi = [own_field(far1, 3 + k) for k in range(3)]
-    rho = SIGMA / (smooth * smooth * smooth) * sums[...] + (1.0 - live)
-    rho = jnp.where(low, rho, 1.0)
-    vol = mass / rho
-    press = GAMMA_LESS * own_e[0:B] / rho
-    rho_ref[...] = rho[:, 0:W]
-
-    def packed(value):
-        return jnp.concatenate([value[0:HALF, 0:W], value[HALF:B, 0:W]], axis=1)
-
-    pack_b[0:HALF, :] = packed(vol)
-    pack_b[HALF:B, :] = jnp.zeros((HALF, 128), F32)
-    b_go()
+    to_smem(1).start()
+    to_smem(1).wait()
     reg_b[here] = pack_b[...]
 
     def blocks_of(body):
@@ -386,6 +428,9 @@
 
     lax.fori_loop(0, B, slopes, 0)
 
+    near_out()
+    a_out()
+    wide_out()
     b_in()
 
     @pl.when(dom == 0)
@@ -455,6 +500,8 @@
             heat = term if heat is None else heat + term
     energy = own_e[0:B] + STEP_DT * SLOPE * (live * press * heat)
 
+    b_out()
+    c_out()
     c_in()
 
     @pl.when(dom == 0)
@@ -494,11 +541,6 @@
     out_ref[pl.ds((7) * B, B), :] = smooth[:, 0:W]
     out_ref[pl.ds((8) * B, B), :] = energy[:, 0:W]
 
-    meta_out()
-    a_out()
-    b_out()
-    c_out()
-
 
 def local(sizes, state, counts, neighbours, new_place):
     D, G = sizes
@@ -507,7 +549,7 @@
     tiles = (NBR + 2) // 2
     half = blocks // 2
     vmem = pl.BlockSpec(memory_space=pltpu.VMEM)
-    smem = pl.BlockSpec(memory_space=pltpu.SMEM)
+    hbm = pl.BlockSpec(memory_space=pltpu.HBM)
     sems = pltpu.SemaphoreType.DMA((3 * G,))
     moved, rho = pl.pallas_call(
         functools.partial(kernel, (D, G, NBR)),
@@ -515,7 +557,7 @@
             jax.ShapeDtypeStruct((9 * blocks, width), F32),
             jax.ShapeDtypeStruct((blocks, width), F32),
         ),
-        in_specs=[vmem, vmem, smem, smem],
+        in_specs=[hbm] * 4,
         out_specs=(vmem, vmem),
         scratch_shapes=[
             pltpu.VMEM((8, 128), jnp.int32),
@@ -530,7 +572,9 @@
             pltpu.SMEM((2, 8, 128), jnp.int32),
             pltpu.VMEM((blocks * tiles * 8, 128), F32),
             pltpu.VMEM((blocks * tiles * 8, 128), F32),
-            pltpu.VMEM((4, width, 128), F32),
+            pltpu.VMEM((blocks, 4, width, 128), F32),
+            pltpu.VMEM((blocks, 8, 128), F32),
+            pltpu.VMEM((blocks, width, 128), F32),
             pltpu.VMEM((blocks, width, 128), F32),
             pltpu.VMEM((blocks, width, tiles * 128), F32),
             pltpu.VMEM((SPLITS, blocks, width, tiles * 128), BF16),
@@ -540,11 +584,16 @@
             pltpu.VMEM((blocks * 32, 128), F32),
             pltpu.VMEM((blocks * 32, 128), F32),
             pltpu.VMEM((4, SPLITS * 32, tiles * 128), BF16),
+            pltpu.VMEM((9 * blocks, width), F32),
+            pltpu.VMEM((blocks, NBR), jnp.int32),
+            pltpu.SMEM((blocks,), jnp.int32),
+            pltpu.SMEM((blocks,), jnp.int32),
+            pltpu.SemaphoreType.DMA((4,)),
             pltpu.SemaphoreType.DMA,
         ]
         + [sems] * 8,
         compiler_params=pltpu.CompilerParams(
-            collective_id=0, has_side_effects=True, vmem_limit_bytes=40 * 2**20
+            collective_id=0, has_side_effects=True, vmem_limit_bytes=56 * 2**20
         ),
     )(
         jnp.transpose(state, (1, 0, 2)).reshape(9 * blocks, width),

time: 56.7 us -> 53.3 us (0.940)
  Pallas kernels: 52.5 us -> 50.4 us
  local copies, waits for them, and re-layouts: 3.32 us -> 1.98 us
    pallas_call x1, Pallas kernels: 52.5 us -> 50.4 us  [local(): pl.pallas_call(functools.partial(kernel, (D, G, NBR)), out_shape=(jax.Sha...]
    unnamed x10 -> x4, local copies, waits for them, and re-layouts: 3.32 us -> 1.98 us
where the time goes in v3:
time: 53.3 us; the launch traced here: 53 us
  Pallas kernels  50.4 us (95%)
  local copies, waits for them, and re-layouts  1.98 us (4%)
  between operations  0.65 us (1%)
    pallas_call x1, Pallas kernels, local(): pl.pallas_call(functools.partial(kernel, (D, G, NBR)), out_shape=(jax.Sha...  50.4 us
    unnamed x4, local copies, waits for them, and re-layouts  1.98 us

profile of v3, /device:TPU:1, one launch (start us, length us, event | category | flops | bytes accessed | tf_op | source)
XLA Modules:
  0.0 53.0 jit_solution(3226255346421888923)
XLA Ops:
  0.6 50.4 %shard_map.59 = (f32[72,64]{1,0:T(8,128)}, f32[8,64]{1,0:T(8,128)}) custom-call(f32[72,64]{1,0:T(8,128)} %bitcast.6, s32[8,26]{1,0:T(8,128)} %nb_hbm.1, s32[8]{0:T(128)} %counts_hbm.1, s32[8]{0:T(128)} %place_hbm.1), custom_call_target="tpu_custom_call" | custom-call | tf_op jit(solution)/shard_map/pallas_call | solution.py:554
  51.0 0.0 copy-start
  51.0 1.4 %copy.8 = f32[8,9,64]{2,0,1:T(8,128)} copy(f32[8,9,64]{2,0,1:T(8,128)} %bitcast.7) | data formatting | bytes 36864
  52.4 0.0 copy-done
  52.4 0.6 %copy.9 = f32[8,64]{1,0:T(8,128)} copy(f32[8,64]{1,0:T(8,128)S(1)} %copy-done) | data formatting | bytes 4096
Async XLA Ops:
  51.0 1.4 %copy-start = (f32[8,64]{1,0:T(8,128)S(1)}, f32[8,64]{1,0:T(8,128)}, u32[]{:S(2)}) copy-start(f32[8,64]{1,0:T(8,128)} %get-tuple-element.9) | copy-start | bytes 6148

commit v4 on v3

--- a/solution.py
+++ b/solution.py
@@ -374,11 +374,11 @@
 
     def blocks_of(body):
         def several(i, c):
-            for k in range(4):
-                body(i * 4 + k, k)
+            for k in range(8):
+                body(i * 8 + k, k)
             return c
 
-        lax.fori_loop(0, B // 4, several, 0)
+        lax.fori_loop(0, B // 8, several, 0)
 
     def store_moment(k, t, value, way):
         at = pl.ds(pl.multiple_of(t * 128, 128), 128)
@@ -583,7 +583,7 @@
             pltpu.VMEM((blocks * 32, 128), F32),
             pltpu.VMEM((blocks * 32, 128), F32),
             pltpu.VMEM((blocks * 32, 128), F32),
-            pltpu.VMEM((4, SPLITS * 32, tiles * 128), BF16),
+            pltpu.VMEM((8, SPLITS * 32, tiles * 128), BF16),
             pltpu.VMEM((9 * blocks, width), F32),
             pltpu.VMEM((blocks, NBR), jnp.int32),
             pltpu.SMEM((blocks,), jnp.int32),

time: 53.3 us -> 52.7 us (0.989)
  Pallas kernels: 50.4 us -> 49.8 us
    pallas_call x1, Pallas kernels: 50.4 us -> 49.8 us  [local(): pl.pallas_call(functools.partial(kernel, (D, G, NBR)), out_shape=(jax.Sha...]
where the time goes in v4:
time: 52.7 us; the launch traced here: 52.4 us
  Pallas kernels  49.8 us (94%)
  local copies, waits for them, and re-layouts  1.98 us (4%)
  between operations  0.65 us (1%)
    pallas_call x1, Pallas kernels, local(): pl.pallas_call(functools.partial(kernel, (D, G, NBR)), out_shape=(jax.Sha...  49.8 us
    unnamed x4, local copies, waits for them, and re-layouts  1.98 us

profile of v4, /device:TPU:1, one launch (start us, length us, event | category | flops | bytes accessed | tf_op | source)
XLA Modules:
  0.0 52.4 jit_solution(13129675245283485570)
XLA Ops:
  0.6 49.8 %shard_map.59 = (f32[72,64]{1,0:T(8,128)}, f32[8,64]{1,0:T(8,128)}) custom-call(f32[72,64]{1,0:T(8,128)} %bitcast.6, s32[8,26]{1,0:T(8,128)} %nb_hbm.1, s32[8]{0:T(128)} %counts_hbm.1, s32[8]{0:T(128)} %place_hbm.1), custom_call_target="tpu_custom_call" | custom-call | tf_op jit(solution)/shard_map/pallas_call | solution.py:554
  50.4 0.0 copy-start
  50.4 1.4 %copy.8 = f32[8,9,64]{2,0,1:T(8,128)} copy(f32[8,9,64]{2,0,1:T(8,128)} %bitcast.7) | data formatting | bytes 36864
  51.8 0.0 copy-done
  51.8 0.6 %copy.9 = f32[8,64]{1,0:T(8,128)} copy(f32[8,64]{1,0:T(8,128)S(1)} %copy-done) | data formatting | bytes 4096
Async XLA Ops:
  50.4 1.4 %copy-start = (f32[8,64]{1,0:T(8,128)S(1)}, f32[8,64]{1,0:T(8,128)}, u32[]{:S(2)}) copy-start(f32[8,64]{1,0:T(8,128)} %get-tuple-element.9) | copy-start | bytes 6148
